TPU v7x, 512 devices: a whole 4x8x8 slice. The times are simulated.
512 devices in a mesh: row: 32 (over y, x), layer: 16 (over z, core).
Axes of the slice: x: 4, y: 8, z: 8, core: 2. Of those that a mesh axis runs over, the one named last changes fastest.
Arguments:
- panel_left: bfloat16 [32, 32, 2048, 128], P('row', 'layer'), may hold values from -6 to 6
- panel_right: bfloat16 [32, 32, 2048, 128], P('row', 'layer'), may hold values from -0.125 to 0.125
- test_matrix: bfloat16 [2048, 128], replicated, may hold values from -6 to 6
- ranks: int32 [32, 32], P('row', 'layer'), may hold values from 32 to 128, as said below
- offsets: int32 [32, 2], P('row'), may hold values from 1 to 4, as said below
Outputs:
- basis: float32 [32, 2048, 2, 128], P('row', 'layer')
- update_right: float32 [32, 2048, 2, 128], P('row', 'layer')
Inputs may be any that keep to these rules, and one draw needn't show every extreme that they name: `ranks`: some tile has rank 128 and some tile has rank 128 // 4. An owner's 2 offsets differ from each other; the values 1 and 4 occur in every draw.
All inputs are finite; a program needn't handle non-finite values.
Results may differ from a plain program's by a relative error of at most 0.0003.
Values may be sent and summed in bfloat16 or wider, within the bound.
A program may use at most 64 MiB of HBM per device.

v0:
```python
import jax
import jax.numpy as jnp
from jax import lax
from jax.sharding import PartitionSpec as P

FRONTS = 4
TARGETS = 2


def passed_along(x, axis, by):
    length = lax.axis_size(axis)
    return lax.ppermute(x, axis, [(i, (i + by) % length) for i in range(length)])


def constant_of(front_item):
    return lambda: front_item


def orthonormal(sketch_rows, gram_mat):
    factor = jnp.linalg.cholesky(gram_mat)
    by_cols = jnp.transpose(sketch_rows, (1, 2, 0))
    solved = lax.linalg.triangular_solve(factor, by_cols, left_side=True, lower=True)
    return jnp.transpose(solved, (2, 0, 1))


def gram_of(sketch_rows, tile_size):
    return (
        jnp.einsum("bsr,bsq->srq", sketch_rows, sketch_rows, precision=lax.Precision.HIGHEST)
        / tile_size
    )


def on_device(panel_left, panel_right, test_matrix, ranks, offsets):
    high = lax.Precision.HIGHEST
    tile_size = panel_left.shape[2]
    rank_cap = panel_left.shape[3]
    share_rows = tile_size // lax.axis_size("layer")
    columns = lax.broadcasted_iota(jnp.int32, (ranks.shape[1], 1, rank_cap), 2)
    live_cols = (columns < ranks[0][:, None, None]).astype(jnp.bfloat16)
    own_left = panel_left[0] * live_cols
    own_right = panel_right[0] * live_cols
    stacked = jnp.stack([own_left, own_right])
    fronts = []
    moving = stacked
    for step_no in range(FRONTS):
        moving = passed_along(moving, "row", 1)
        fronts.append(moving)
    branches = [constant_of(front_item) for front_item in fronts]
    left_full = own_left.astype(jnp.float32)
    cores = []
    mixers = []
    partners = []
    for target in range(TARGETS):
        partner = lax.switch(offsets[0, target] - 1, branches)
        core_mat = jnp.einsum(
            "kbr,kbq->krq", own_right, partner[1], preferred_element_type=jnp.float32
        )
        probes = jnp.einsum(
            "kbr,bq->krq", partner[0], test_matrix, preferred_element_type=jnp.float32
        )
        mix_mat = jnp.einsum("krq,kqs->krs", core_mat, probes, precision=high)
        cores.append(core_mat)
        mixers.append(mix_mat)
        partners.append(partner[0].astype(jnp.float32))
    mixed = jnp.stack(mixers, axis=1)
    local_sketch = jnp.einsum("kbr,ksrq->bsq", left_full, mixed, precision=high)
    total_sketch = lax.psum(local_sketch, "layer")
    basis_all = orthonormal(total_sketch, gram_of(total_sketch, tile_size))
    first_own = lax.axis_index("layer") * share_rows
    basis_part = lax.dynamic_slice_in_dim(basis_all, first_own, share_rows, 0)
    reach = jnp.einsum("kbr,bsq->ksrq", left_full, basis_all, precision=high)
    weights = []
    for target in range(TARGETS):
        weight_mat = jnp.einsum("krq,krs->kqs", cores[target], reach[:, target], precision=high)
        weights.append(weight_mat)
    term_list = []
    for target in range(TARGETS):
        row_piece = lax.slice_in_dim(
            partners[target], 0, share_rows * lax.axis_size("layer"), axis=1
        )
        term_list.append(jnp.einsum("kbq,kqs->bs", row_piece, weights[target], precision=high))
    update_right = lax.psum_scatter(
        jnp.stack(term_list, axis=1) / tile_size, "layer", scatter_dimension=0, tiled=True
    )
    return (basis_part[None], update_right[None])


def solution(mesh):
    return jax.shard_map(
        on_device,
        mesh=mesh,
        in_specs=(
            P("row", "layer", None, None),
            P("row", "layer", None, None),
            P(),
            P("row", "layer"),
            P("row", None),
        ),
        out_specs=(P("row", "layer", None, None), P("row", "layer", None, None)),
        check_vma=False,
    )
```

profile of v0, /device:TPU:2, one launch (start us, length us, event | category | flops | bytes accessed | tf_op | source)
XLA Modules:
  0.0 479.9 jit_solution(14630520279900826652)
XLA Ops:
  7.2 0.8 compare_convert_fusion
  8.0 1.7 broadcast_multiply_fusion.1
  9.9 3.4 collective-permute-start
  13.3 45.9 %collective-permute-done = bf16[2,2,2048,128]{3,2,1,0:T(8,128)(2,1)S(1)} collective-permute-done((bf16[2,2,2048,128]{3,2,1,0:T(8,128)(2,1)S(1)}, bf16[2,2,2048,128]{3,2,1,0:T(8,128)(2,1)S(1)}, u32[]{:S(2)}, u32[]{:S(2)}) %collective-permute-start) | collective-permute-done | bytes 2097184 | tf_op jit(solution)/shard_map/ppermute | solution.py:12
  59.2 3.4 collective-permute-start.1
  62.6 44.0 %collective-permute-done.1 = bf16[2,2,2048,128]{3,2,1,0:T(8,128)(2,1)S(1)} collective-permute-done((bf16[2,2,2048,128]{3,2,1,0:T(8,128)(2,1)S(1)}, bf16[2,2,2048,128]{3,2,1,0:T(8,128)(2,1)S(1)}, u32[]{:S(2)}, u32[]{:S(2)}) %collective-permute-start.1) | collective-permute-done | bytes 2097184 | tf_op jit(solution)/shard_map/ppermute | solution.py:12
  106.6 4.4 collective-permute-start.2
  110.9 43.6 %collective-permute-done.2 = bf16[2,2,2048,128]{3,2,1,0:T(8,128)(2,1)} collective-permute-done((bf16[2,2,2048,128]{3,2,1,0:T(8,128)(2,1)S(1)}, bf16[2,2,2048,128]{3,2,1,0:T(8,128)(2,1)}, u32[]{:S(2)}, u32[]{:S(2)}) %collective-permute-start.2) | collective-permute-done | bytes 2097184 | tf_op jit(solution)/shard_map/ppermute | solution.py:12
  154.5 4.0 collective-permute-start.3
  158.5 0.6 fusion.27
  160.4 41.0 %collective-permute-done.3 = bf16[2,2,2048,128]{3,2,1,0:T(8,128)(2,1)} collective-permute-done((bf16[2,2,2048,128]{3,2,1,0:T(8,128)(2,1)}, bf16[2,2,2048,128]{3,2,1,0:T(8,128)(2,1)}, u32[]{:S(2)}, u32[]{:S(2)}) %collective-permute-start.3) | collective-permute-done | bytes 2097184 | tf_op jit(solution)/shard_map/ppermute | solution.py:12
  201.4 3.1 conditional.2
  201.4 3.1 copy.36
  204.5 2.0 fusion.8
  206.5 2.2 fusion.7
  208.8 0.5 fusion.11
  209.4 0.5 fusion.12
  210.4 2.3 convolution_bitcast_fusion
  213.0 138.5 %all-reduce.2.cloned.1.call-done = f32[2048,2,128]{2,0,1:T(8,128)} async-done(((f32[2048,2,128]{2,0,1:T(8,128)}), f32[2048,2,128]{2,0,1:T(8,128)}) %all-reduce.2.cloned.1.call-update) | async-done | bytes 2097168 | tf_op jit(solution)/shard_map/psum | solution.py:67
  351.6 5.8 %fusion.28 = f32[2,128,128]{2,1,0:T(8,128)S(1)} fusion(f32[2048,2,128]{2,0,1:T(8,128)} %all-reduce.2.cloned.1.call-done), kind=kOutput, calls=%fused_computation.51 | convolution fusion | flops 805306368 | bytes 2228224 | tf_op jit(solution)/shard_map/bsr,bsq->srq/dot_general | solution.py:28
  357.5 23.5 %custom-call.7 = f32[2,128,128]{2,1,0:T(8,128)S(1)} custom-call(f32[2,128,128]{2,1,0:T(8,128)S(1)} %fusion.25), custom_call_target="Cholesky" | custom-call | tf_op jit(solution)/shard_map/jit(cholesky)/cholesky | solution.py:20
  381.2 19.9 %custom-call.8 = f32[2,1,128,128]{2,3,1,0:T(8,128)S(1)} custom-call(f32[2,1,128,128]{3,2,1,0:T(8,128)S(1)} %select_bitcast_fusion), custom_call_target="InvertDiagBlocksLowerTriangular" | custom-call | tf_op jit(solution)/shard_map/triangular_solve | solution.py:22
  401.2 2.0 fusion.2
  403.1 1.2 fusion.4
  404.3 0.4 fusion.22
  405.5 1.0 convolution_bitcast_fusion.1
  406.5 1.0 convolution_bitcast_fusion.2
  407.5 1.4 maximum_multiply_fusion
  409.0 0.9 dynamic-slice_bitcast_fusion
  409.9 0.8 copy.21
  410.7 60.7 %reduce-scatter.2.cloned.1.call-done = f32[128,2,128]{2,0,1:T(8,128)} async-done(((f32[2048,2,128]{2,0,1:T(8,128)}), f32[128,2,128]{2,0,1:T(8,128)}) %reduce-scatter.2.cloned.1.call-update) | async-done | bytes 131088 | tf_op jit(solution)/shard_map/reduce_scatter | solution.py:82
  471.4 1.7 copy.22
  (38 shorter events, 2.4 us)
Async XLA Ops:
  7.2 201.6 %copy-start = (bf16[2048,128]{1,0:T(8,128)(2,1)S(1)}, bf16[2048,128]{1,0:T(8,128)(2,1)}, u32[]{:S(2)}) copy-start(bf16[2048,128]{1,0:T(8,128)(2,1)} %param.15) | copy-start | bytes 1572868
  7.2 344.4 %all-reduce.2.cloned.1.call-start = ((), (), s32[]{:S(2)}) async-start(), calls=%async_computation.1 | async-start | bytes 4194304 | tf_op jit(solution)/shard_map/psum | solution.py:67
  9.7 148.8 %copy-start.10 = (s32[1,2]{1,0:T(1,128)S(1)}, s32[1,2]{1,0:T(1,128)}, u32[]{:S(2)}) copy-start(s32[1,2]{1,0:T(1,128)} %param.17) | copy-start | bytes 28
  9.9 49.3 %collective-permute-start = (bf16[2,2,2048,128]{3,2,1,0:T(8,128)(2,1)S(1)}, bf16[2,2,2048,128]{3,2,1,0:T(8,128)(2,1)S(1)}, u32[]{:S(2)}, u32[]{:S(2)}) collective-permute-start(bf16[2,2,2048,128]{3,2,1,0:T(8,128)(2,1)S(1)} %pad_maximum_fusion), channel_id=1, source_target_pairs={{0,16},{16,32},{32,48},{48,64},{64,80},{80,96},{96,112},{112,128},... | collective-permute-start | bytes 6291464 | tf_op jit(solution)/shard_map/ppermute | solution.py:12
  59.2 142.2 %copy-start.5 = (bf16[2,2,2048,128]{3,2,1,0:T(8,128)(2,1)}, bf16[2,2,2048,128]{3,2,1,0:T(8,128)(2,1)S(1)}, u32[]{:S(2)}) copy-start(bf16[2,2,2048,128]{3,2,1,0:T(8,128)(2,1)S(1)} %collective-permute-done) | copy-start | bytes 6291460
  59.2 47.4 %collective-permute-start.1 = (bf16[2,2,2048,128]{3,2,1,0:T(8,128)(2,1)S(1)}, bf16[2,2,2048,128]{3,2,1,0:T(8,128)(2,1)S(1)}, u32[]{:S(2)}, u32[]{:S(2)}) collective-permute-start(bf16[2,2,2048,128]{3,2,1,0:T(8,128)(2,1)S(1)} %collective-permute-done), channel_id=1, source_target_pairs={{0,16},{16,32},{32,48},{48,64},{64,80},{80,96},{96,112},{112,128},... | collective-permute-start | bytes 6291464 | tf_op jit(solution)/shard_map/ppermute | solution.py:12
  106.6 48.0 %collective-permute-start.2 = (bf16[2,2,2048,128]{3,2,1,0:T(8,128)(2,1)S(1)}, bf16[2,2,2048,128]{3,2,1,0:T(8,128)(2,1)}, u32[]{:S(2)}, u32[]{:S(2)}) collective-permute-start(bf16[2,2,2048,128]{3,2,1,0:T(8,128)(2,1)S(1)} %collective-permute-done.1), channel_id=1, source_target_pairs={{0,16},{16,32},{32,48},{48,64},{64,80},{80,96},{96,112},{112,128},... | collective-permute-start | bytes 6291464 | tf_op jit(solution)/shard_map/ppermute | solution.py:12
  154.5 46.9 %collective-permute-start.3 = (bf16[2,2,2048,128]{3,2,1,0:T(8,128)(2,1)}, bf16[2,2,2048,128]{3,2,1,0:T(8,128)(2,1)}, u32[]{:S(2)}, u32[]{:S(2)}) collective-permute-start(bf16[2,2,2048,128]{3,2,1,0:T(8,128)(2,1)} %collective-permute-done.2), channel_id=1, source_target_pairs={{0,16},{16,32},{32,48},{48,64},{64,80},{80,96},{96,112},{112,128},... | collective-permute-start | bytes 6291464 | tf_op jit(solution)/shard_map/ppermute | solution.py:12
  206.5 2.2 copy-start.8
  206.5 2.8 copy-start.6
  208.7 1.7 copy-start.2
  212.8 258.6 %reduce-scatter.2.cloned.1.call-start = ((), (), s32[]{:S(2)}) async-start(), calls=%async_computation.2 | async-start | bytes 2228224 | tf_op jit(solution)/shard_map/reduce_scatter | solution.py:82
  351.6 49.6 %copy-start.1 = (f32[2048,2,128]{2,0,1:T(8,128)S(1)}, f32[2048,2,128]{2,0,1:T(8,128)}, u32[]{:S(2)}) copy-start(f32[2048,2,128]{2,0,1:T(8,128)} %all-reduce.2.cloned.1.call-done) | copy-start | bytes 6291460
  401.1 2.0 copy-start.3
  403.1 2.0 copy-start.4
  403.1 2.3 copy-start.7
  404.3 2.2 copy-start.9
Sparse Core Ops, SparseCore 0:
  212.9 138.6 all-reduce.1
  409.1 62.2 reduce-scatter.1
where the time goes:
time: 480 us
  waiting for transfers between devices  374 us (78%)
  other arithmetic  47.7 us (10%)
  matrix products  19.8 us (4%)
  between operations  15.7 us (3%)
  starting transfers between devices  15.4 us (3%)
  local copies, waits for them, and re-layouts  7.61 us (2%)
    ppermute x4, waiting for transfers between devices, passed_along(): lax.ppermute(x, axis, [(i, (i + by) % length) for i in range(length)])  174 us
    psum x1, waiting for transfers between devices, on_device(): total_sketch = lax.psum(local_sketch, 'layer')  139 us
    reduce_scatter x1, waiting for transfers between devices, on_device(): lax.psum_scatter(jnp.stack(term_list, axis=1) / tile_size, 'layer', scatt...  60.7 us
    another operation x4, other arithmetic, orthonormal(): factor = jnp.linalg.cholesky(gram_mat)  23.6 us
    another operation x3, other arithmetic, orthonormal(): lax.linalg.triangular_solve(factor, by_cols, left_side=True, lower=True)  20 us
    ppermute x4, starting transfers between devices, passed_along(): lax.ppermute(x, axis, [(i, (i + by) % length) for i in range(length)])  15.1 us
  transfers between devices with their start and end apart: 6, of which 6 were waited for; matrix products, arithmetic and copies ran while one was open for 0% of the time, Pallas kernels for 0%

commit v1 on v0

--- a/solution.py
+++ b/solution.py
@@ -64,7 +64,7 @@
         partners.append(partner[0].astype(jnp.float32))
     mixed = jnp.stack(mixers, axis=1)
     local_sketch = jnp.einsum("kbr,ksrq->bsq", left_full, mixed, precision=high)
-    total_sketch = lax.psum(local_sketch, "layer")
+    total_sketch = jnp.sum(lax.all_gather(local_sketch, "layer"), axis=0)
     basis_all = orthonormal(total_sketch, gram_of(total_sketch, tile_size))
     first_own = lax.axis_index("layer") * share_rows
     basis_part = lax.dynamic_slice_in_dim(basis_all, first_own, share_rows, 0)

time: 480 us -> 546 us (1.14)
  waiting for transfers between devices: 374 us -> 429 us
  other arithmetic: 47.7 us -> 59.5 us
    all_gather x0 -> x1, waiting for transfers between devices: none -> 195 us  [on_device(): total_sketch = jnp.sum(lax.all_gather(local_sketch, 'layer'), axis=0)]
    psum x1 -> x0, waiting for transfers between devices: 139 us -> none  [on_device(): total_sketch = lax.psum(local_sketch, 'layer')]
    reduce_sum x0 -> x1, other arithmetic: none -> 11.8 us  [on_device(): total_sketch = jnp.sum(lax.all_gather(local_sketch, 'layer'), axis=0)]
where the time goes in v1:
time: 546 us; the launch traced here: 545 us
  waiting for transfers between devices  429 us (79%)
  other arithmetic  59.5 us (11%)
  matrix products  18.8 us (3%)
  between operations  15.6 us (3%)
  starting transfers between devices  15.4 us (3%)
  local copies, waits for them, and re-layouts  7.45 us (1%)
    all_gather x1, waiting for transfers between devices, on_device(): total_sketch = jnp.sum(lax.all_gather(local_sketch, 'layer'), axis=0)  195 us
    ppermute x4, waiting for transfers between devices, passed_along(): lax.ppermute(x, axis, [(i, (i + by) % length) for i in range(length)])  174 us
    reduce_scatter x1, waiting for transfers between devices, on_device(): lax.psum_scatter(jnp.stack(term_list, axis=1) / tile_size, 'layer', scatt...  59.2 us
    another operation x4, other arithmetic, orthonormal(): factor = jnp.linalg.cholesky(gram_mat)  23.6 us
    another operation x3, other arithmetic, orthonormal(): lax.linalg.triangular_solve(factor, by_cols, left_side=True, lower=True)  20 us
    ppermute x4, starting transfers between devices, passed_along(): lax.ppermute(x, axis, [(i, (i + by) % length) for i in range(length)])  15.1 us
    reduce_sum x1, other arithmetic, on_device(): total_sketch = jnp.sum(lax.all_gather(local_sketch, 'layer'), axis=0)  11.8 us
  transfers between devices with their start and end apart: 6, of which 6 were waited for; matrix products, arithmetic and copies ran while one was open for 0% of the time, Pallas kernels for 0%

profile of v1, /device:TPU:2, one launch (start us, length us, event | category | flops | bytes accessed | tf_op | source)
XLA Modules:
  0.0 545.5 jit_solution(13776478301894709389)
XLA Ops:
  7.2 0.8 compare_convert_fusion
  8.0 1.7 broadcast_multiply_fusion.1
  9.9 3.4 collective-permute-start
  13.3 45.9 %collective-permute-done = bf16[2,2,2048,128]{3,2,1,0:T(8,128)(2,1)S(1)} collective-permute-done((bf16[2,2,2048,128]{3,2,1,0:T(8,128)(2,1)S(1)}, bf16[2,2,2048,128]{3,2,1,0:T(8,128)(2,1)S(1)}, u32[]{:S(2)}, u32[]{:S(2)}) %collective-permute-start) | collective-permute-done | bytes 2097184 | tf_op jit(solution)/shard_map/ppermute | solution.py:12
  59.2 3.4 collective-permute-start.1
  62.6 44.0 %collective-permute-done.1 = bf16[2,2,2048,128]{3,2,1,0:T(8,128)(2,1)S(1)} collective-permute-done((bf16[2,2,2048,128]{3,2,1,0:T(8,128)(2,1)S(1)}, bf16[2,2,2048,128]{3,2,1,0:T(8,128)(2,1)S(1)}, u32[]{:S(2)}, u32[]{:S(2)}) %collective-permute-start.1) | collective-permute-done | bytes 2097184 | tf_op jit(solution)/shard_map/ppermute | solution.py:12
  106.6 4.4 collective-permute-start.2
  110.9 43.6 %collective-permute-done.2 = bf16[2,2,2048,128]{3,2,1,0:T(8,128)(2,1)} collective-permute-done((bf16[2,2,2048,128]{3,2,1,0:T(8,128)(2,1)S(1)}, bf16[2,2,2048,128]{3,2,1,0:T(8,128)(2,1)}, u32[]{:S(2)}, u32[]{:S(2)}) %collective-permute-start.2) | collective-permute-done | bytes 2097184 | tf_op jit(solution)/shard_map/ppermute | solution.py:12
  154.5 4.0 collective-permute-start.3
  158.5 0.6 fusion.27
  160.4 41.0 %collective-permute-done.3 = bf16[2,2,2048,128]{3,2,1,0:T(8,128)(2,1)} collective-permute-done((bf16[2,2,2048,128]{3,2,1,0:T(8,128)(2,1)}, bf16[2,2,2048,128]{3,2,1,0:T(8,128)(2,1)}, u32[]{:S(2)}, u32[]{:S(2)}) %collective-permute-start.3) | collective-permute-done | bytes 2097184 | tf_op jit(solution)/shard_map/ppermute | solution.py:12
  201.4 3.0 conditional.2
  201.4 3.0 copy.59
  204.4 2.2 fusion.8
  206.6 0.5 fusion.11
  207.2 2.1 fusion.7
  209.3 1.7 fusion.12
  211.5 2.4 convolution_bitcast_fusion
  214.2 195.1 %all-gather.3.cloned.1.call-done = f32[32768,2,128]{2,0,1:T(8,128)} async-done(((f32[2048,2,128]{2,0,1:T(8,128)}), f32[32768,2,128]{2,0,1:T(8,128)}) %all-gather.3.cloned.1.call-update) | async-done | bytes 33554448 | tf_op jit(solution)/shard_map/all_gather | solution.py:67
  409.3 11.8 %reduce_sum.9 = f32[2048,2,128]{2,0,1:T(8,128)S(1)} reduce(f32[16,2048,2,128]{3,1,0,2:T(8,128)} %bitcast.101, f32[]{:T(128)} %constant.64.clone.1), dimensions={0}, to_apply=%region_8.0 | reduce | flops 7864320 | bytes 35651588 | tf_op jit(solution)/shard_map/reduce_sum | solution.py:67
  421.1 3.5 fusion.28
  424.7 23.5 %custom-call.7 = f32[2,128,128]{2,1,0:T(8,128)S(1)} custom-call(f32[2,128,128]{2,1,0:T(8,128)S(1)} %fusion.25), custom_call_target="Cholesky" | custom-call | tf_op jit(solution)/shard_map/jit(cholesky)/cholesky | solution.py:20
  448.4 19.9 %custom-call.8 = f32[2,1,128,128]{2,3,1,0:T(8,128)S(1)} custom-call(f32[2,1,128,128]{3,2,1,0:T(8,128)S(1)} %select_bitcast_fusion), custom_call_target="InvertDiagBlocksLowerTriangular" | custom-call | tf_op jit(solution)/shard_map/triangular_solve | solution.py:22
  468.3 2.0 fusion.2
  470.3 1.2 fusion.4
  472.6 1.0 convolution_bitcast_fusion.2
  473.6 1.0 convolution_bitcast_fusion.1
  474.6 1.5 maximum_multiply_fusion
  476.1 0.9 dynamic-slice_bitcast_fusion
  477.1 0.8 copy.36
  477.8 59.2 %reduce-scatter.2.cloned.1.call-done = f32[128,2,128]{2,0,1:T(8,128)} async-done(((f32[2048,2,128]{2,0,1:T(8,128)}), f32[128,2,128]{2,0,1:T(8,128)}) %reduce-scatter.2.cloned.1.call-update) | async-done | bytes 131088 | tf_op jit(solution)/shard_map/reduce_scatter | solution.py:82
  537.0 1.7 copy.37
  (35 shorter events, 2.6 us)
Async XLA Ops:
  7.2 199.4 %copy-start = (bf16[2048,128]{1,0:T(8,128)(2,1)S(1)}, bf16[2048,128]{1,0:T(8,128)(2,1)}, u32[]{:S(2)}) copy-start(bf16[2048,128]{1,0:T(8,128)(2,1)} %param.15) | copy-start | bytes 1572868
  7.2 402.1 %all-gather.3.cloned.1.call-start = ((), (), s32[]{:S(2)}) async-start(), calls=%async_computation.2 | async-start | bytes 35651584 | tf_op jit(solution)/shard_map/all_gather | solution.py:67
  9.7 148.8 %copy-start.8 = (s32[1,2]{1,0:T(1,128)S(1)}, s32[1,2]{1,0:T(1,128)}, u32[]{:S(2)}) copy-start(s32[1,2]{1,0:T(1,128)} %param.17) | copy-start | bytes 28
  9.9 49.3 %collective-permute-start = (bf16[2,2,2048,128]{3,2,1,0:T(8,128)(2,1)S(1)}, bf16[2,2,2048,128]{3,2,1,0:T(8,128)(2,1)S(1)}, u32[]{:S(2)}, u32[]{:S(2)}) collective-permute-start(bf16[2,2,2048,128]{3,2,1,0:T(8,128)(2,1)S(1)} %pad_maximum_fusion), channel_id=1, source_target_pairs={{0,16},{16,32},{32,48},{48,64},{64,80},{80,96},{96,112},{112,128},... | collective-permute-start | bytes 6291464 | tf_op jit(solution)/shard_map/ppermute | solution.py:12
  59.2 142.2 %copy-start.4 = (bf16[2,2,2048,128]{3,2,1,0:T(8,128)(2,1)}, bf16[2,2,2048,128]{3,2,1,0:T(8,128)(2,1)S(1)}, u32[]{:S(2)}) copy-start(bf16[2,2,2048,128]{3,2,1,0:T(8,128)(2,1)S(1)} %collective-permute-done) | copy-start | bytes 6291460
  59.2 47.4 %collective-permute-start.1 = (bf16[2,2,2048,128]{3,2,1,0:T(8,128)(2,1)S(1)}, bf16[2,2,2048,128]{3,2,1,0:T(8,128)(2,1)S(1)}, u32[]{:S(2)}, u32[]{:S(2)}) collective-permute-start(bf16[2,2,2048,128]{3,2,1,0:T(8,128)(2,1)S(1)} %collective-permute-done), channel_id=1, source_target_pairs={{0,16},{16,32},{32,48},{48,64},{64,80},{80,96},{96,112},{112,128},... | collective-permute-start | bytes 6291464 | tf_op jit(solution)/shard_map/ppermute | solution.py:12
  106.6 48.0 %collective-permute-start.2 = (bf16[2,2,2048,128]{3,2,1,0:T(8,128)(2,1)S(1)}, bf16[2,2,2048,128]{3,2,1,0:T(8,128)(2,1)}, u32[]{:S(2)}, u32[]{:S(2)}) collective-permute-start(bf16[2,2,2048,128]{3,2,1,0:T(8,128)(2,1)S(1)} %collective-permute-done.1), channel_id=1, source_target_pairs={{0,16},{16,32},{32,48},{48,64},{64,80},{80,96},{96,112},{112,128},... | collective-permute-start | bytes 6291464 | tf_op jit(solution)/shard_map/ppermute | solution.py:12
  154.5 46.9 %collective-permute-start.3 = (bf16[2,2,2048,128]{3,2,1,0:T(8,128)(2,1)}, bf16[2,2,2048,128]{3,2,1,0:T(8,128)(2,1)}, u32[]{:S(2)}, u32[]{:S(2)}) collective-permute-start(bf16[2,2,2048,128]{3,2,1,0:T(8,128)(2,1)} %collective-permute-done.2), channel_id=1, source_target_pairs={{0,16},{16,32},{32,48},{48,64},{64,80},{80,96},{96,112},{112,128},... | collective-permute-start | bytes 6291464 | tf_op jit(solution)/shard_map/ppermute | solution.py:12
  204.4 2.2 copy-start.6
  207.2 4.4 copy-start.1
  214.0 323.0 %reduce-scatter.2.cloned.1.call-start = ((), (), s32[]{:S(2)}) async-start(), calls=%async_computation.1 | async-start | bytes 2228224 | tf_op jit(solution)/shard_map/reduce_scatter | solution.py:82
  468.3 2.0 copy-start.2
  470.3 2.0 copy-start.3
  470.3 2.3 copy-start.7
  471.5 2.2 copy-start.5
Sparse Core Ops, SparseCore 0:
  214.1 195.1 all-gather.2
  476.3 60.6 reduce-scatter.1
